TPU v7x, 128 devices: a whole 4x4x4 slice. The times are simulated.
128 devices in a mesh: ctx: 32 (over y, x_lo, z), dp: 4 (over x_hi, core).
Axes of the slice: x: 4 (x_hi: 2, x_lo: 2; x = x_hi * 2 + x_lo), y: 4, z: 4, core: 2. Of those that a mesh axis runs over, the one named last changes fastest.
Arguments:
- query_raw: bfloat16 [4, 16384, 2048], P('dp', 'ctx'), may hold values from -6 to 6
- key_raw: bfloat16 [4, 16384, 1024], P('dp', 'ctx'), may hold values from -6 to 6
- values: bfloat16 [4, 16384, 1024], P('dp', 'ctx'), may hold values from -6 to 6
- out_grad: bfloat16 [4, 16384, 2048], P('dp', 'ctx'), may hold values from -36 to 36
- query_scale: float32 [128], replicated, may hold values from 0.5 to 6
- key_scale: float32 [128], replicated, may hold values from 0.5 to 6
- block_doc: int32 [4, 16], P('dp'), may hold values from 0 to 14, as said below
- doc_end: int32 [4, 16], P('dp'), may hold values from 0 to 16384, as said below
Outputs:
- attended: bfloat16 [4, 16384, 2048], P('dp', 'ctx')
- query_grad: bfloat16 [4, 16384, 2048], P('dp', 'ctx')
- key_grad: bfloat16 [4, 16384, 1024], P('dp', 'ctx')
- value_grad: bfloat16 [4, 16384, 1024], P('dp', 'ctx')
- query_scale_grad: float32 [128], replicated
- key_scale_grad: float32 [128], replicated
Inputs may be any that keep to these rules, and one draw needn't show every extreme that they name: `block_doc`: along each sequence the document id is 0 in the first block and rises by 0 or 1 from block to block; documents start at multiples of 1024. In every draw one sequence starts a new document at every block but the second. `doc_end`: entry d is one past the last real token of document d; the rest of the document's last block is padding; the last document of a sequence ends at 16384; unused entries are 0.
All inputs are finite; a program needn't handle non-finite values.
Results may differ from a plain program's by a relative error of at most 0.0035.
The roundings to bfloat16 on the way count: a program that leaves them out, or rounds other values in their place, can miss the bound.
Values may be sent and summed in bfloat16 or wider, within the bound.
A program may use at most 192 MiB of HBM per device.

v0:
```python
import jax
import jax.numpy as jnp
from jax import lax
from jax.sharding import PartitionSpec as P

WINDOW = 1024
BLOCK = 1024


score_scale = 168.0 ** (-0.5)
norm_eps = 1e-06


def shifted(block, axis, distance):
    devices = range(lax.axis_size(axis))
    route = [(i - distance, i) for i in devices if i - distance in devices]
    return lax.ppermute(block, axis, route)


def head_norm(inputs, scales):
    mean_square = jnp.mean(inputs * inputs, axis=-1, keepdims=True)
    return inputs * lax.rsqrt(mean_square + norm_eps) * scales


def lookup(entries, wanted):
    places = lax.iota(jnp.int32, entries.shape[0])
    return jnp.sum(jnp.where(places == wanted, entries, 0))


def shard_facts(query_shard, offset, doc_row, end_row, shard_rows, shards):
    source = query_shard - offset
    query_doc = lookup(doc_row, query_shard * shard_rows // BLOCK)
    source_doc = lookup(doc_row, source * shard_rows // BLOCK)
    live_flag = (source >= 0) & (query_shard < shards) & (source_doc == query_doc)
    return (live_flag, source * shard_rows, lookup(end_row, source_doc))


def tile_mask(offset, live_flag, key_start, key_limit, tile_rows):
    query_place = lax.broadcasted_iota(jnp.int32, (tile_rows, tile_rows), 0)
    key_place = lax.broadcasted_iota(jnp.int32, (tile_rows, tile_rows), 1)
    distance = offset * tile_rows + query_place - key_place
    inside = (distance >= 0) & (distance < WINDOW)
    usable = key_start + key_place < key_limit
    return inside & usable & live_flag


def dot_rows(former, latter):
    return lax.dot_general(
        former, latter, (((1,), (1,)), ((), ())), preferred_element_type=jnp.float32
    )


def dot_cols(former, latter):
    return lax.dot_general(
        former, latter, (((0,), (0,)), ((), ())), preferred_element_type=jnp.float32
    )


def soft_parts(scores):
    row_peak = jnp.max(scores, axis=1, keepdims=True)
    log_total = row_peak + jnp.log(jnp.sum(jnp.exp(scores - row_peak), axis=1, keepdims=True))
    return (log_total, jnp.exp(scores - log_total))


def head_pass(query_head, grad_head, key_tiles, value_tiles, tile_masks):
    tile_count, tile_rows, head_dim = key_tiles.shape
    group_rows = query_head.shape[0]
    group_size = group_rows // tile_rows
    row_masks = [
        jnp.tile(tile_masks[tile_slot], (group_size, 1)) for tile_slot in range(tile_count)
    ]
    key_flat = key_tiles.reshape(tile_count * tile_rows, head_dim)
    value_flat = value_tiles.reshape(tile_count * tile_rows, head_dim)
    raw_scores = dot_rows(query_head, key_flat) * score_scale
    log_total, shares = soft_parts(
        jnp.where(jnp.concatenate(row_masks, axis=1), raw_scores, -jnp.inf)
    )
    weights = shares.astype(jnp.bfloat16)
    attended = jnp.dot(weights, value_flat, preferred_element_type=jnp.float32).astype(jnp.bfloat16)
    row_delta = jnp.sum(
        grad_head.astype(jnp.float32) * attended.astype(jnp.float32), axis=1, keepdims=True
    )
    share_grad = dot_rows(grad_head, value_flat)
    score_grad = (shares * (share_grad - row_delta) * score_scale).astype(jnp.bfloat16)
    query_grad = jnp.dot(score_grad, key_flat, preferred_element_type=jnp.float32)
    key_grads = dot_cols(score_grad, query_head).reshape(tile_count, tile_rows, head_dim)
    value_grads = dot_cols(weights, grad_head).reshape(tile_count, tile_rows, head_dim)
    return (attended, query_grad, key_grads, value_grads, log_total[:, 0], row_delta[:, 0])


def body(query_raw, key_raw, values, out_grad, query_scale, key_scale, block_doc, doc_end):
    tile_rows = query_raw.shape[1]
    head_dim = query_scale.shape[0]
    head_count = query_raw.shape[2] // head_dim
    key_heads = key_raw.shape[2] // head_dim
    group_size = head_count // key_heads
    shard_index = lax.axis_index("ctx")
    shards = lax.axis_size("ctx")
    query_float = query_raw[0].astype(jnp.float32).reshape(tile_rows, head_count, head_dim)
    key_float = key_raw[0].astype(jnp.float32).reshape(tile_rows, key_heads, head_dim)
    query_norm = head_norm(query_float, query_scale).astype(jnp.bfloat16)
    key_norm = (
        head_norm(key_float, key_scale)
        .astype(jnp.bfloat16)
        .reshape(tile_rows, key_heads * head_dim)
    )
    own_pair = (key_norm, values[0])
    arrived = []
    for distance in (1, 2):
        arrived.append(shifted((own_pair[0], own_pair[1]), "ctx", distance))
    key_stack = jnp.stack([arrived[1][0], arrived[0][0], own_pair[0]])
    value_stack = jnp.stack([arrived[1][1], arrived[0][1], own_pair[1]])
    key_tiles = key_stack.reshape(3, tile_rows, key_heads, head_dim).transpose(2, 0, 1, 3)
    value_tiles = value_stack.reshape(3, tile_rows, key_heads, head_dim).transpose(2, 0, 1, 3)
    doc_row = block_doc[0]
    end_row = doc_end[0]
    mask_list = []
    live_flags = []
    for offset in (2, 1, 0):
        live_flag, key_start, key_limit = shard_facts(
            shard_index, offset, doc_row, end_row, tile_rows, shards
        )
        live_flags.append(live_flag)
        mask_list.append(tile_mask(offset, live_flag, key_start, key_limit, tile_rows))
    tile_masks = jnp.stack(mask_list)
    query_heads = (
        query_norm.reshape(tile_rows, key_heads, group_size, head_dim)
        .transpose(1, 2, 0, 3)
        .reshape(key_heads, group_size * tile_rows, head_dim)
    )
    grad_heads = (
        out_grad[0]
        .reshape(tile_rows, key_heads, group_size, head_dim)
        .transpose(1, 2, 0, 3)
        .reshape(key_heads, group_size * tile_rows, head_dim)
    )

    def per_head(operands):
        return head_pass(operands[0], operands[1], operands[2], operands[3], tile_masks)

    attended_heads, query_grad_heads, key_parts, value_parts, log_totals, row_deltas = lax.map(
        per_head, (query_heads, grad_heads, key_tiles, value_tiles)
    )
    key_total = key_parts[:, -1]
    value_total = value_parts[:, -1]
    for distance in (1, 2):
        outgoing = (
            key_parts[:, 2 - distance].astype(jnp.bfloat16),
            value_parts[:, 2 - distance].astype(jnp.bfloat16),
        )
        incoming = shifted((outgoing[0], outgoing[1]), "ctx", -distance)
        key_total = key_total + incoming[0].astype(jnp.float32)
        value_total = value_total + incoming[1].astype(jnp.float32)
    attended = (
        attended_heads.reshape(key_heads, group_size, tile_rows, head_dim)
        .transpose(2, 0, 1, 3)
        .reshape(1, tile_rows, head_count * head_dim)
    )
    query_norm_grad = (
        query_grad_heads.reshape(key_heads, group_size, tile_rows, head_dim)
        .transpose(2, 0, 1, 3)
        .reshape(tile_rows, head_count, head_dim)
    )
    normed, query_pull = jax.vjp(head_norm, query_float, query_scale)
    query_in_grad, query_scale_part = query_pull(query_norm_grad)
    normed, key_pull = jax.vjp(head_norm, key_float, key_scale)
    key_in_grad, key_scale_part = key_pull(key_total.transpose(1, 0, 2))
    scale_totals = lax.psum(
        (
            jnp.sum(query_scale_part.reshape(1, head_dim), axis=0),
            jnp.sum(key_scale_part.reshape(1, head_dim), axis=0),
        ),
        ("ctx", "dp"),
    )
    value_grad = (
        value_total.transpose(1, 0, 2)
        .reshape(1, tile_rows, key_heads * head_dim)
        .astype(jnp.bfloat16)
    )
    query_grad = query_in_grad.astype(jnp.bfloat16).reshape(1, tile_rows, head_count * head_dim)
    key_grad = key_in_grad.astype(jnp.bfloat16).reshape(1, tile_rows, key_heads * head_dim)
    return (attended, query_grad, key_grad, value_grad, scale_totals[0], scale_totals[1])


def solution(mesh):
    in_specs = (
        P("dp", "ctx", None),
        P("dp", "ctx", None),
        P("dp", "ctx", None),
        P("dp", "ctx", None),
        P(),
        P(),
        P("dp", None),
        P("dp", None),
    )
    out_specs = (
        P("dp", "ctx", None),
        P("dp", "ctx", None),
        P("dp", "ctx", None),
        P("dp", "ctx", None),
        P(),
        P(),
    )
    return jax.shard_map(body, mesh=mesh, in_specs=in_specs, out_specs=out_specs, check_vma=False)
```

profile of v0, /device:TPU:0, one launch (start us, length us, event | category | flops | bytes accessed | tf_op | source)
XLA Modules:
  0.0 621.3 jit_solution(403186728259900940)
XLA Ops:
  5.8 6.9 %collective-permute-start = (bf16[512,1024]{0,1:T(8,128)(2,1)}, bf16[512,1024]{0,1:T(8,128)(2,1)}, u32[]{:S(2)}, u32[]{:S(2)}) collective-permute-start(bf16[512,1024]{0,1:T(8,128)(2,1)} %fusion.49), channel_id=1, source_target_pairs={{0,8},{4,12},{8,16},{12,20},{16,24},{20,28},{24,32},{28,36},{32,40... | collective-permute-start | bytes 3145736 | tf_op jit(solution)/shard_map/ppermute | solution.py:17
  21.9 4.8 collective-permute-start.3
  29.1 5.2 reshape.253
  42.2 7.6 %fusion.41 = bf16[8,2,512,128]{3,1,0,2:T(2,128)(2,1)} fusion(f32[512,8,2,128]{3,2,1,0:T(2,128)} %reshape.253, f32[128]{0:T(128)S(1)} %copy-done.25, f32[512,8,2]{2,1,0:T(8,128)S(1)} %copy.68), kind=kLoop, calls=%fused_computation.62 | loop fusion | flops 3145728 | bytes 6324736 | tf_op jit(solution)/shard_map/transpose | solution.py:128
  61.0 8.4 %copy.73 = bf16[512,8,2,128]{0,2,3,1:T(2,128)(2,1)S(1)} copy(bf16[512,8,2,128]{3,2,1,0:T(2,128)(2,1)} %reshape_squeeze.3) | data formatting | bytes 4194304 | tf_op jit(solution)/shard_map/reshape;squeeze | solution.py:133
  74.7 5.0 mul.245
  88.5 13.3 %collective-permute-done.3 = bf16[512,1024]{0,1:T(8,128)(2,1)} collective-permute-done((bf16[512,1024]{0,1:T(8,128)(2,1)}, bf16[512,1024]{0,1:T(8,128)(2,1)}, u32[]{:S(2)}, u32[]{:S(2)}) %collective-permute-start.3) | collective-permute-done | bytes 1048608 | tf_op jit(solution)/shard_map/ppermute | solution.py:17
  105.4 282.7 %while.17 = (s32[]{:T(128)}, bf16[8,1024,128]{1,2,0:T(8,128)(2,1)}, f32[8,1024,128]{2,1,0:T(8,128)}, f32[8,3,512,128]{2,3,0,1:T(8,128)}, f32[8,3,512,128]{3,2,1,...) while((s32[]{:T(128)}, bf16[8,1024,128]{1,2,0:T(8,128)(2,1)}, ...), condition=%wide.region_12.13_spmd.clone, body=%wide.region_8.0_spmd.clone.sunk | while | flops 2446456832 | bytes 131659696 | solution.py:141
  122.5 4.9 bitcast_dynamic-update-slice_fusion.2
  157.7 4.9 bitcast_dynamic-update-slice_fusion.2
  193.0 4.9 bitcast_dynamic-update-slice_fusion.2
  228.4 4.9 bitcast_dynamic-update-slice_fusion.2
  263.7 4.9 bitcast_dynamic-update-slice_fusion.2
  299.0 4.9 bitcast_dynamic-update-slice_fusion.2
  334.2 4.9 bitcast_dynamic-update-slice_fusion.2
  369.5 4.9 bitcast_dynamic-update-slice_fusion.2
  388.1 10.9 %multiply_reduce_fusion.1 = f32[128]{0:T(128)S(1)} fusion(f32[512,8,2,128]{3,2,1,0:T(2,128)} %reshape.253, f32[512,8,2]{2,1,0:T(8,128)} %copy-done.9, f32[8,2,512,128]{3,2,1,0:T(8,128)} %bitcast.213), kind=kLoop, calls=%fused_computation.54 | loop fusion | flops 3145600 | bytes 8421888 | tf_op jit(solution)/shard_map/transpose(jvp())/reduce_sum | solution.py:22
  418.4 4.9 broadcast_in_dim.56
  423.3 6.4 %reshape.250 = f32[1,512,2048]{2,1,0:T(8,128)} reshape(f32[512,8,2,128]{3,2,1,0:T(2,128)} %bitcast.209) | data formatting | bytes 8388608 | tf_op jit(solution)/shard_map/reshape | solution.py:162
  433.1 6.4 %copy.76 = bf16[8,2,512,128]{3,1,0,2:T(2,128)(2,1)} copy(bf16[8,2,512,128]{2,1,3,0:T(2,128)(2,1)S(1)} %reshape.247) | data formatting | bytes 4194304 | tf_op jit(solution)/shard_map/reshape | solution.py:155
  439.5 4.6 reshape.248
  444.1 7.7 %fusion.39 = bf16[1,512,2048]{2,1,0:T(8,128)(2,1)} fusion(f32[1,512,2048]{2,1,0:T(8,128)} %broadcast_in_dim.56, f32[1,512,2048]{2,1,0:T(8,128)} %mul.245, f32[1,512,2048]{2,1,0:T(8,128)} %reshape.250, bf16[1,512,2048]{2,1,0:T(8,128)(2,1)S(1)} %copy-done.7, f32[2048]{0:T(1024)S(1)} %copy-done.20), kind=kLoop, calls=%fused_computation.53 | loop fusion | flops 7340032 | bytes 16785408 | tf_op jit(solution)/shard_map/convert_element_type | solution.py:180
  451.8 45.0 %collective-permute-done.6 = bf16[8,512,128]{2,1,0:T(8,128)(2,1)S(1)} collective-permute-done((bf16[8,512,128]{2,1,0:T(8,128)(2,1)}, bf16[8,512,128]{2,1,0:T(8,128)(2,1)S(1)}, u32[]{:S(2)}, u32[]{:S(2)}) %collective-permute-start.6) | collective-permute-done | bytes 1048608 | tf_op jit(solution)/shard_map/ppermute | solution.py:17
  508.6 112.4 %all-reduce = (f32[128]{0:T(128)}, f32[128]{0:T(128)}) all-reduce(f32[128]{0:T(128)S(1)} %multiply_reduce_fusion.1, f32[128]{0:T(128)S(1)} %get-tuple-element.190), channel_id=1, replica_groups=mesh['ctx'=32,'dp'=4] {'ctx','dp'}, use_global_device_ids=true, to_apply=%region_16.17 | all-reduce | flops 256 | bytes 2048 | tf_op jit(solution)/shard_map/psum | solution.py:168
  (417 shorter events, 327.1 us)
Async XLA Ops:
  2.1 24.5 %copy-start.6 = (bf16[1,512,2048]{2,1,0:T(8,128)(2,1)S(1)}, bf16[1,512,2048]{2,1,0:T(8,128)(2,1)}, u32[]{:S(2)}) copy-start(bf16[1,512,2048]{2,1,0:T(8,128)(2,1)} %param.10) | copy-start | bytes 6291460
  4.5 45.3 %copy-start.14 = (f32[512,8]{0,1:T(8,128)}, f32[512,8]{0,1:T(8,128)S(1)}, u32[]{:S(2)}) copy-start(f32[512,8]{0,1:T(8,128)S(1)} %fusion.52) | copy-start | bytes 49156
  5.8 79.1 %collective-permute-start = (bf16[512,1024]{0,1:T(8,128)(2,1)}, bf16[512,1024]{0,1:T(8,128)(2,1)}, u32[]{:S(2)}, u32[]{:S(2)}) collective-permute-start(bf16[512,1024]{0,1:T(8,128)(2,1)} %fusion.49), channel_id=1, source_target_pairs={{0,8},{4,12},{8,16},{12,20},{16,24},{20,28},{24,32},{28,36},{32,40... | collective-permute-start | bytes 3145736 | tf_op jit(solution)/shard_map/ppermute | solution.py:17
  12.6 72.2 %collective-permute-start.1 = (bf16[512,1024]{0,1:T(8,128)(2,1)}, bf16[512,1024]{0,1:T(8,128)(2,1)}, u32[]{:S(2)}, u32[]{:S(2)}) collective-permute-start(bf16[512,1024]{0,1:T(8,128)(2,1)} %fusion.49), channel_id=1, source_target_pairs={{0,4},{4,8},{8,12},{12,16},{16,20},{20,24},{24,28},{28,32},{32,36}... | collective-permute-start | bytes 3145736 | tf_op jit(solution)/shard_map/ppermute | solution.py:17
  18.8 69.7 %collective-permute-start.2 = (bf16[512,1024]{0,1:T(8,128)(2,1)}, bf16[512,1024]{0,1:T(8,128)(2,1)}, u32[]{:S(2)}, u32[]{:S(2)}) collective-permute-start(bf16[512,1024]{0,1:T(8,128)(2,1)} %bitcast.221), channel_id=1, source_target_pairs={{0,8},{4,12},{8,16},{12,20},{16,24},{20,28},{24,32},{28,36},{32,40... | collective-permute-start | bytes 3145736 | tf_op jit(solution)/shard_map/ppermute | solution.py:17
  21.9 80.0 %collective-permute-start.3 = (bf16[512,1024]{0,1:T(8,128)(2,1)}, bf16[512,1024]{0,1:T(8,128)(2,1)}, u32[]{:S(2)}, u32[]{:S(2)}) collective-permute-start(bf16[512,1024]{0,1:T(8,128)(2,1)} %bitcast.222), channel_id=1, source_target_pairs={{0,4},{4,8},{8,12},{12,16},{16,20},{20,24},{24,28},{28,32},{32,36}... | collective-permute-start | bytes 3145736 | tf_op jit(solution)/shard_map/ppermute | solution.py:17
  74.7 10.1 %copy-start.13 = (bf16[1,512,1024]{1,2,0:T(8,128)(2,1)S(1)}, bf16[1,512,1024]{1,2,0:T(8,128)(2,1)}, u32[]{:S(2)}) copy-start(bf16[1,512,1024]{1,2,0:T(8,128)(2,1)} %fusion.47) | copy-start | bytes 3145732
  84.8 17.0 %copy-start.12 = (bf16[1,512,1024]{1,2,0:T(8,128)(2,1)S(1)}, bf16[1,512,1024]{1,2,0:T(8,128)(2,1)}, u32[]{:S(2)}) copy-start(bf16[1,512,1024]{1,2,0:T(8,128)(2,1)} %copy.71) | copy-start | bytes 3145732
  118.3 10.1 %slice-start = ((s8[6291456]{0:T(1024)(128)(4,1)}), s8[2097152]{0:T(1024)(128)(4,1)S(1)}, s32[]{:S(2)}) async-start(s8[6291456]{0:T(1024)(128)(4,1)} %bitcast.197), calls=%async_computation | async-start | bytes 4194304 | tf_op jit(solution)/shard_map/while
  153.6 10.1 %slice-start = ((s8[6291456]{0:T(1024)(128)(4,1)}), s8[2097152]{0:T(1024)(128)(4,1)S(1)}, s32[]{:S(2)}) async-start(s8[6291456]{0:T(1024)(128)(4,1)} %bitcast.197), calls=%async_computation | async-start | bytes 4194304 | tf_op jit(solution)/shard_map/while
  188.8 10.1 %slice-start = ((s8[6291456]{0:T(1024)(128)(4,1)}), s8[2097152]{0:T(1024)(128)(4,1)S(1)}, s32[]{:S(2)}) async-start(s8[6291456]{0:T(1024)(128)(4,1)} %bitcast.197), calls=%async_computation | async-start | bytes 4194304 | tf_op jit(solution)/shard_map/while
  224.2 10.1 %slice-start = ((s8[6291456]{0:T(1024)(128)(4,1)}), s8[2097152]{0:T(1024)(128)(4,1)S(1)}, s32[]{:S(2)}) async-start(s8[6291456]{0:T(1024)(128)(4,1)} %bitcast.197), calls=%async_computation | async-start | bytes 4194304 | tf_op jit(solution)/shard_map/while
  259.5 10.1 %slice-start = ((s8[6291456]{0:T(1024)(128)(4,1)}), s8[2097152]{0:T(1024)(128)(4,1)S(1)}, s32[]{:S(2)}) async-start(s8[6291456]{0:T(1024)(128)(4,1)} %bitcast.197), calls=%async_computation | async-start | bytes 4194304 | tf_op jit(solution)/shard_map/while
  294.8 10.1 %slice-start = ((s8[6291456]{0:T(1024)(128)(4,1)}), s8[2097152]{0:T(1024)(128)(4,1)S(1)}, s32[]{:S(2)}) async-start(s8[6291456]{0:T(1024)(128)(4,1)} %bitcast.197), calls=%async_computation | async-start | bytes 4194304 | tf_op jit(solution)/shard_map/while
  330.1 10.0 %slice-start = ((s8[6291456]{0:T(1024)(128)(4,1)}), s8[2097152]{0:T(1024)(128)(4,1)S(1)}, s32[]{:S(2)}) async-start(s8[6291456]{0:T(1024)(128)(4,1)} %bitcast.197), calls=%async_computation | async-start | bytes 4194304 | tf_op jit(solution)/shard_map/while
  365.3 10.1 %slice-start = ((s8[6291456]{0:T(1024)(128)(4,1)}), s8[2097152]{0:T(1024)(128)(4,1)S(1)}, s32[]{:S(2)}) async-start(s8[6291456]{0:T(1024)(128)(4,1)} %bitcast.197), calls=%async_computation | async-start | bytes 4194304 | tf_op jit(solution)/shard_map/while
  388.0 14.2 %slice-start.2 = ((s8[6291456]{0:T(1024)(128)(4,1)}), s8[4194304]{0:T(1024)(128)(4,1)S(1)}, s32[]{:S(2)}) async-start(s8[6291456]{0:T(1024)(128)(4,1)} %bitcast.210), calls=%async_computation.2 | async-start | bytes 8388608
  388.0 10.9 %copy-start.10 = (f32[8,1024,128]{2,1,0:T(8,128)S(1)}, f32[8,1024,128]{2,1,0:T(8,128)}, u32[]{:S(2)}) copy-start(f32[8,1024,128]{2,1,0:T(8,128)} %get-tuple-element.72) | copy-start | bytes 12582916
  388.1 14.2 %slice-start.3 = ((s8[6291456]{0:T(1024)(128)(4,1)}), s8[2097152]{0:T(1024)(128)(4,1)S(1)}, s32[]{:S(2)}) async-start(s8[6291456]{0:T(1024)(128)(4,1)} %bitcast.210), calls=%async_computation.3 | async-start | bytes 4194304
  402.2 11.9 %copy-start.5 = (f32[8,2,512,128]{3,1,0,2:T(2,128)}, f32[8,2,512,128]{3,1,0,2:T(2,128)S(1)}, u32[]{:S(2)}) copy-start(f32[8,2,512,128]{3,1,0,2:T(2,128)S(1)} %copy.106) | copy-start | bytes 12582916
  404.7 96.4 %collective-permute-start.4 = (bf16[8,512,128]{1,2,0:T(8,128)(2,1)}, bf16[8,512,128]{1,2,0:T(8,128)(2,1)}, u32[]{:S(2)}, u32[]{:S(2)}) collective-permute-start(bf16[8,512,128]{1,2,0:T(8,128)(2,1)} %get-tuple-element.248), channel_id=1, source_target_pairs={{4,0},{8,4},{12,8},{16,12},{20,16},{24,20},{28,24},{32,28},{36,32}... | collective-permute-start | bytes 3145736 | tf_op jit(solution)/shard_map/ppermute | solution.py:17
  406.2 94.8 %collective-permute-start.5 = (bf16[8,512,128]{1,2,0:T(8,128)(2,1)}, bf16[8,512,128]{1,2,0:T(8,128)(2,1)}, u32[]{:S(2)}, u32[]{:S(2)}) collective-permute-start(bf16[8,512,128]{1,2,0:T(8,128)(2,1)} %get-tuple-element.249), channel_id=1, source_target_pairs={{8,0},{12,4},{16,8},{20,12},{24,16},{28,20},{32,24},{36,28},{40,32... | collective-permute-start | bytes 3145736 | tf_op jit(solution)/shard_map/ppermute | solution.py:17
  411.5 85.3 %collective-permute-start.6 = (bf16[8,512,128]{2,1,0:T(8,128)(2,1)}, bf16[8,512,128]{2,1,0:T(8,128)(2,1)S(1)}, u32[]{:S(2)}, u32[]{:S(2)}) collective-permute-start(bf16[8,512,128]{2,1,0:T(8,128)(2,1)} %get-tuple-element.246), channel_id=1, source_target_pairs={{4,0},{8,4},{12,8},{16,12},{20,16},{24,20},{28,24},{32,28},{36,32}... | collective-permute-start | bytes 3145736 | tf_op jit(solution)/shard_map/ppermute | solution.py:17
  412.8 84.0 %collective-permute-start.7 = (bf16[8,512,128]{2,1,0:T(8,128)(2,1)}, bf16[8,512,128]{2,1,0:T(8,128)(2,1)}, u32[]{:S(2)}, u32[]{:S(2)}) collective-permute-start(bf16[8,512,128]{2,1,0:T(8,128)(2,1)} %get-tuple-element.247), channel_id=1, source_target_pairs={{8,0},{12,4},{16,8},{20,12},{24,16},{28,20},{32,24},{36,28},{40,32... | collective-permute-start | bytes 3145736 | tf_op jit(solution)/shard_map/ppermute | solution.py:17
  (82 other events, 322.5 us)
where the time goes:
time: 632 us; the launch traced here: 621 us
  local copies, waits for them, and re-layouts  167 us (26%)
  matrix products  166 us (26%)
  blocking collectives  112 us (18%)
  other arithmetic  88.2 us (14%)
  waiting for transfers between devices  58.3 us (9%)
  starting transfers between devices  24 us (4%)
    psum x1, blocking collectives, body(): lax.psum((jnp.sum(query_scale_part.reshape(1, head_dim), axis=0), jnp.sum...  112 us
    ppermute x8, waiting for transfers between devices, shifted(): return lax.ppermute(block, axis, route)  58.3 us
    dot_general x16, matrix products, dot_cols(): lax.dot_general(former, latter, (((0,), (0,)), ((), ())), preferred_eleme...  56.9 us
    dot_general x16, matrix products, dot_rows(): lax.dot_general(former, latter, (((1,), (1,)), ((), ())), preferred_eleme...  55.8 us
    dot_general x16, local copies, waits for them, and re-layouts, dot_cols(): lax.dot_general(former, latter, (((0,), (0,)), ((), ())), preferred_eleme...  48.4 us
    dot_general x8, matrix products, head_pass(): jnp.dot(weights, value_flat, preferred_element_type=jnp.float32)  38.9 us
    ppermute x8, starting transfers between devices, shifted(): return lax.ppermute(block, axis, route)  24 us
    dynamic_slice x24, local copies, waits for them, and re-layouts, body(): lax.map(per_head, (query_heads, grad_heads, key_tiles, value_tiles))  19 us
  transfers between devices with their start and end apart: 8, of which 2 were waited for; matrix products, arithmetic and copies ran while one was open for 17% of the time, Pallas kernels for 0%

commit v1 on v0

v1 whole, which is shorter than its diff:
```python
import functools

import jax
import jax.numpy as jnp
from jax import lax
from jax.experimental import pallas as pl
from jax.experimental.pallas import tpu as pltpu
from jax.sharding import PartitionSpec as P

WINDOW = 1024
BLOCK = 1024
MESH = pl.DeviceIdType.MESH
F32 = jnp.float32
BF16 = jnp.bfloat16

score_scale = 168.0 ** (-0.5)
LOG2E = 1.4426950408889634
norm_eps = 1e-06
MASKED = -1e30

HD = 128
T = 512
QB = 256
KB = 256
SPAN = WINDOW + QB
VMEM_LIMIT = 48 * 1024 * 1024


def dot(a, b):
    return lax.dot_general(a, b, (((1,), (0,)), ((), ())), preferred_element_type=F32)


def fold_rows(x, op):
    return op(x.reshape(x.shape[0] // 8, 8, x.shape[1]), axis=0)


def kernel(
    heads,
    ctx_size,
    dp_size,
    inner,
    q_hbm,
    k_hbm,
    v_hbm,
    do_hbm,
    qs_ref,
    ks_ref,
    doc_ref,
    end_ref,
    att_hbm,
    dq_hbm,
    dk_hbm,
    dv_hbm,
    qsg_ref,
    ksg_ref,
    qbuf,
    dobuf,
    kvbuf,
    attbuf,
    dqbuf,
    dkvout,
    kn,
    knt,
    vt,
    khat,
    qst,
    s_buf,
    p_buf,
    ds_buf,
    dkacc,
    dvacc,
    own,
    g2send,
    g1buf,
    g2recv,
    g1recv,
    qsacc,
    ksacc,
    ar1,
    ar2,
    ar3,
    load_sem,
    store_sem,
    a_send,
    a_recv,
    r_send,
    r_recv,
    g2_send,
    g2_recv,
    g1_send,
    g1_recv,
    ar_send,
    ar_recv,
):
    me = lax.axis_index("ctx")
    dp = lax.axis_index("dp")
    nxt = lax.rem(me + 1, ctx_size)
    prv = lax.rem(me + ctx_size - 1, ctx_size)
    outer = ctx_size // inner
    me_in = lax.rem(me, inner)
    me_out = me // inner

    def load_copies(h):
        wide = pl.ds(pl.multiple_of(h * 2 * HD, 2 * HD), 2 * HD)
        narrow = pl.ds(pl.multiple_of(h * HD, HD), HD)
        return (
            pltpu.make_async_copy(k_hbm.at[:, narrow], kvbuf.at[h, 0, pl.ds(2 * T, T)], load_sem.at[h, 0]),
            pltpu.make_async_copy(v_hbm.at[:, narrow], kvbuf.at[h, 1, pl.ds(2 * T, T)], load_sem.at[h, 1]),
            pltpu.make_async_copy(q_hbm.at[:, wide], qbuf.at[h], load_sem.at[h, 2]),
            pltpu.make_async_copy(do_hbm.at[:, wide], dobuf.at[h], load_sem.at[h, 3]),
        )

    def query_stores(h):
        wide = pl.ds(pl.multiple_of(h * 2 * HD, 2 * HD), 2 * HD)
        return (
            pltpu.make_async_copy(attbuf.at[h], att_hbm.at[:, wide], store_sem.at[h, 0]),
            pltpu.make_async_copy(dqbuf.at[h], dq_hbm.at[:, wide], store_sem.at[h, 1]),
        )

    def key_stores(h):
        narrow = pl.ds(pl.multiple_of(h * HD, HD), HD)
        return (
            pltpu.make_async_copy(dkvout.at[h, 0], dk_hbm.at[:, narrow], store_sem.at[h, 2]),
            pltpu.make_async_copy(dkvout.at[h, 1], dv_hbm.at[:, narrow], store_sem.at[h, 3]),
        )

    def remote(src, dst, send, recv, device):
        return pltpu.make_async_remote_copy(
            src_ref=src, dst_ref=dst, send_sem=send, recv_sem=recv, device_id=device, device_id_type=MESH
        )

    def halo_near(h):
        narrow = pl.ds(pl.multiple_of(h * HD, HD), HD)
        near = pl.ds(T, T)
        return (
            remote(k_hbm.at[:, narrow], kvbuf.at[h, 0, near], a_send.at[h, 0], a_recv.at[h, 0], {"ctx": nxt}),
            remote(v_hbm.at[:, narrow], kvbuf.at[h, 1, near], a_send.at[h, 1], a_recv.at[h, 1], {"ctx": nxt}),
        )

    def halo_far(h):
        return remote(
            kvbuf.at[h, :, pl.ds(T, T)], kvbuf.at[h, :, pl.ds(0, T)], r_send.at[h], r_recv.at[h], {"ctx": nxt}
        )

    def grad_far(h):
        return remote(g2send.at[h], g2recv.at[h], g2_send.at[h], g2_recv.at[h], {"ctx": prv})

    def grad_near(h):
        return remote(g1buf.at[h], g1recv.at[h], g1_send.at[h], g1_recv.at[h], {"ctx": prv})

    def partners(stage):
        if stage == 0:
            return [{"dp": lax.rem(dp + d, dp_size)} for d in range(1, dp_size)]
        if stage == 1:
            return [{"ctx": me_out * inner + lax.rem(me_in + d, inner)} for d in range(1, inner)]
        return [{"ctx": lax.rem(me_out + d, outer) * inner + me_in} for d in range(1, outer)]

    stage_slot = (dp, me_in, me_out)
    stage_buf = (ar1, ar2, ar3)
    stage_base = (0, dp_size - 1, dp_size + inner - 2)

    def stage_copies(stage):
        slot = stage_buf[stage].at[stage_slot[stage]]
        base = stage_base[stage]
        return [
            remote(slot, slot, ar_send.at[base + d], ar_recv.at[base + d], device)
            for d, device in enumerate(partners(stage))
        ]

    def stage_start(stage, value):
        stage_buf[stage][stage_slot[stage]] = value
        for copy in stage_copies(stage):
            copy.start()

    def stage_sum(stage):
        for copy in stage_copies(stage):
            copy.wait()
        total = stage_buf[stage][0]
        for slot in range(1, stage_buf[stage].shape[0]):
            total = total + stage_buf[stage][slot]
        return total

    def start_loads(h, carry):
        for copy in load_copies(h):
            copy.start()
        return carry

    lax.fori_loop(0, heads, start_loads, 0)

    barrier = pltpu.get_barrier_semaphore()
    greeted = [{"ctx": nxt}, {"ctx": prv}] + partners(0) + partners(1) + partners(2)
    for device in greeted:
        pl.semaphore_signal(barrier, inc=1, device_id=device, device_id_type=MESH)
    pl.semaphore_wait(barrier, len(greeted))

    def start_halo(h):
        for copy in halo_near(h):
            copy.start()

    for h in range(min(3, heads)):
        start_halo(h)

    qrow = qs_ref[...]
    krow = ks_ref[...]
    half = jnp.transpose(jnp.broadcast_to(qrow, (HD, HD)))
    qst[...] = jnp.concatenate([half, half], axis=1)
    qsacc[...] = jnp.zeros_like(qsacc)
    ksacc[...] = jnp.zeros_like(ksacc)

    block = me * T // BLOCK
    doc = doc_ref[0, block]
    before = doc_ref[0, jnp.maximum(block - 1, 0)]
    same = (block > 0) & (doc == before)
    into = me * T - block * BLOCK
    first = jnp.where(same, 0, 2 * T - into)
    limit = end_ref[0, doc] - (me - 2) * T

    def relay(h):
        for copy in halo_near(h):
            copy.wait_recv()
        halo_far(h).start()

    relay(0)

    def prepare(h):
        def prep_block(b, carry):
            rows = pl.ds(pl.multiple_of(b * KB, KB), KB)
            x = kvbuf[h, 0, rows, :].astype(F32)
            mean_square = jnp.mean(x * x, axis=1, keepdims=True)
            hat = x * lax.rsqrt(mean_square + norm_eps)
            khat[rows, :] = hat
            normed = (hat * krow).astype(BF16)
            kn[rows, :] = normed
            knt[:, rows] = jnp.transpose(normed)
            vt[:, rows] = jnp.transpose(kvbuf[h, 1, rows, :])
            return carry

        lax.fori_loop(0, 3 * T // KB, prep_block, 0)

    def unit(h, g, j):
        rows = pl.ds(j * QB, QB)
        cols = pl.ds(g * HD, HD)
        k0 = j * QB
        nb = SPAN // KB
        gain = qst[...]
        xt = jnp.transpose(qbuf[h, rows, cols].astype(F32))
        mean_square = jnp.mean(xt * xt, axis=0, keepdims=True)
        r = lax.rsqrt(mean_square + norm_eps)
        xr = xt * r
        qt = (xr * gain).astype(BF16)
        do = dobuf[h, rows, cols]
        dot_t = jnp.transpose(do)
        lane = lax.broadcasted_iota(jnp.int32, (1, QB), 1)
        low = jnp.maximum(first, k0 + 1 + lane)
        high = jnp.minimum(limit, k0 + 1 + WINDOW + lane)
        place = lax.broadcasted_iota(jnp.int32, (KB, QB), 0)
        peak = jnp.full((8, QB), MASKED, F32)
        for b in range(nb):
            keys = kn[k0 + b * KB : k0 + (b + 1) * KB, :]
            s = dot(keys, qt)
            spot = place + (k0 + b * KB)
            s = jnp.where((spot >= low) & (spot < high), s, MASKED)
            s_buf[b * KB : (b + 1) * KB, :] = s
            peak = jnp.maximum(peak, fold_rows(s, jnp.max))
        peak = jnp.max(peak, axis=0, keepdims=True)
        total = jnp.zeros((8, QB), F32)
        for b in range(nb):
            e = jnp.exp2((s_buf[b * KB : (b + 1) * KB, :] - peak) * (score_scale * LOG2E))
            s_buf[b * KB : (b + 1) * KB, :] = e
            total = total + fold_rows(e, jnp.sum)
        inverse = 1.0 / jnp.sum(total, axis=0, keepdims=True)
        for b in range(nb):
            p_buf[b * KB : (b + 1) * KB, :] = (s_buf[b * KB : (b + 1) * KB, :] * inverse).astype(BF16)
        o = dot(vt[:, k0 : k0 + SPAN], p_buf[...]).astype(BF16)
        attbuf[h, rows, cols] = jnp.transpose(o)
        delta = jnp.sum(dot_t.astype(F32) * o.astype(F32), axis=0, keepdims=True)
        for b in range(nb):
            part = dot(kvbuf[h, 1, k0 + b * KB : k0 + (b + 1) * KB, :], dot_t)
            shares = s_buf[b * KB : (b + 1) * KB, :] * inverse
            ds_buf[b * KB : (b + 1) * KB, :] = (shares * (part - delta) * score_scale).astype(BF16)
        dqt = dot(knt[:, k0 : k0 + SPAN], ds_buf[...])
        dk = dot(ds_buf[...], jnp.transpose(qt))
        dv = dot(p_buf[...], do)
        if g == 0 and j == 0:
            dkacc[0:SPAN, :] = dk
            dvacc[0:SPAN, :] = dv
        elif g == 0:
            old = SPAN - QB
            dkacc[k0 : k0 + old, :] += dk[:old]
            dvacc[k0 : k0 + old, :] += dv[:old]
            dkacc[k0 + old : k0 + SPAN, :] = dk[old:]
            dvacc[k0 + old : k0 + SPAN, :] = dv[old:]
        else:
            dkacc[k0 : k0 + SPAN, :] += dk
            dvacc[k0 : k0 + SPAN, :] += dv
        gs = dqt * gain
        lean = jnp.mean(gs * xt, axis=0, keepdims=True)
        dx = gs * r - xt * (r * r * r * lean)
        dqbuf[h, rows, cols] = jnp.transpose(dx.astype(BF16))
        qsacc[...] += dqt * xr

    def send_parts(h):
        far_k = dkacc[0:T, :].astype(BF16)
        g2send[h, 0] = far_k
        g2send[h, 1] = dvacc[0:T, :].astype(BF16)
        grad_far(h).start()
        near_k = dkacc[T : 2 * T, :].astype(BF16)
        g1buf[h, 0] = near_k
        g1buf[h, 1] = dvacc[T : 2 * T, :].astype(BF16)
        own_k = dkacc[2 * T : 3 * T, :]
        own[h, 0] = own_k
        own[h, 1] = dvacc[2 * T : 3 * T, :]
        ksacc[...] += (
            fold_rows(far_k.astype(F32) * khat[0:T, :], jnp.sum)
            + fold_rows(near_k.astype(F32) * khat[T : 2 * T, :], jnp.sum)
            + fold_rows(own_k * khat[2 * T : 3 * T, :], jnp.sum)
        )

    def merge(h):
        grad_far(h).wait_recv()
        g1buf[h] = (g1buf[h].astype(F32) + g2recv[h].astype(F32)).astype(BF16)
        grad_near(h).start()

    def finish(h):
        grad_near(h).wait_recv()
        dkvout[h, 1] = (own[h, 1] + g1recv[h, 1].astype(F32)).astype(BF16)
        grad = own[h, 0] + g1recv[h, 0].astype(F32)
        x = kvbuf[h, 0, pl.ds(2 * T, T), :].astype(F32)
        r = lax.rsqrt(jnp.mean(x * x, axis=1, keepdims=True) + norm_eps)
        gs = grad * krow
        lean = jnp.mean(gs * x, axis=1, keepdims=True)
        dkvout[h, 0] = (gs * r - x * (r * r * r * lean)).astype(BF16)
        for copy in key_stores(h):
            copy.start()

    def step(h, carry):
        @pl.when(h + 1 < heads)
        def _():
            relay(h + 1)

        @pl.when(h + 3 < heads)
        def _():
            start_halo(h + 3)

        for copy in load_copies(h):
            copy.wait()
        halo_far(h).wait_recv()
        prepare(h)
        for g in range(2):
            for j in range(T // QB):
                unit(h, g, j)
        send_parts(h)
        for copy in query_stores(h):
            copy.start()

        @pl.when(h >= 1)
        def _():
            merge(h - 1)

        @pl.when(h >= 2)
        def _():
            finish(h - 2)

        return carry

    lax.fori_loop(0, heads, step, 0)

    query_part = jnp.sum(jnp.transpose(qsacc[...]), axis=0, keepdims=True)
    key_part = jnp.sum(ksacc[...], axis=0, keepdims=True)
    row = lax.broadcasted_iota(jnp.int32, (8, HD), 0)
    stage_start(0, jnp.where(row == 0, query_part, jnp.where(row == 1, key_part, 0.0)))
    merge(heads - 1)
    finish(heads - 2)
    stage_start(1, stage_sum(0))
    stage_start(2, stage_sum(1))
    finish(heads - 1)
    totals = stage_sum(2)
    qsg_ref[...] = totals[0:1]
    ksg_ref[...] = totals[1:2]

    def drain(h, carry):
        for copy in halo_near(h):
            copy.wait_send()
        halo_far(h).wait_send()
        grad_far(h).wait_send()
        grad_near(h).wait_send()
        for copy in query_stores(h) + key_stores(h):
            copy.wait()
        return carry

    lax.fori_loop(0, heads, drain, 0)


def body(mesh_shape, query_raw, key_raw, values, out_grad, query_scale, key_scale, block_doc, doc_end):
    ctx_size, dp_size, inner = mesh_shape
    tokens = query_raw.shape[1]
    heads = key_raw.shape[2] // HD
    outer = ctx_size // inner
    exchanges = dp_size + inner + outer - 3
    any_spec = pl.BlockSpec(memory_space=pl.ANY)
    vmem_spec = pl.BlockSpec(memory_space=pltpu.VMEM)
    smem_spec = pl.BlockSpec(memory_space=pltpu.SMEM)
    dma = pltpu.SemaphoreType.DMA
    wide = jax.ShapeDtypeStruct((tokens, 2 * heads * HD), BF16)
    narrow = jax.ShapeDtypeStruct((tokens, heads * HD), BF16)
    gain = jax.ShapeDtypeStruct((1, HD), F32)
    attended, query_grad, key_grad, value_grad, query_gain, key_gain = pl.pallas_call(
        functools.partial(kernel, heads, ctx_size, dp_size, inner),
        out_shape=(wide, wide, narrow, narrow, gain, gain),
        in_specs=[any_spec] * 4 + [vmem_spec] * 2 + [smem_spec] * 2,
        out_specs=[any_spec] * 4 + [vmem_spec] * 2,
        scratch_shapes=[
            pltpu.VMEM((heads, T, 2 * HD), BF16),
            pltpu.VMEM((heads, T, 2 * HD), BF16),
            pltpu.VMEM((heads, 2, 3 * T, HD), BF16),
            pltpu.VMEM((heads, T, 2 * HD), BF16),
            pltpu.VMEM((heads, T, 2 * HD), BF16),
            pltpu.VMEM((heads, 2, T, HD), BF16),
            pltpu.VMEM((3 * T, HD), BF16),
            pltpu.VMEM((HD, 3 * T), BF16),
            pltpu.VMEM((HD, 3 * T), BF16),
            pltpu.VMEM((3 * T, HD), F32),
            pltpu.VMEM((HD, QB), F32),
            pltpu.VMEM((SPAN, QB), F32),
            pltpu.VMEM((SPAN, QB), BF16),
            pltpu.VMEM((SPAN, QB), BF16),
            pltpu.VMEM((3 * T, HD), F32),
            pltpu.VMEM((3 * T, HD), F32),
            pltpu.VMEM((heads, 2, T, HD), F32),
            pltpu.VMEM((heads, 2, T, HD), BF16),
            pltpu.VMEM((heads, 2, T, HD), BF16),
            pltpu.VMEM((heads, 2, T, HD), BF16),
            pltpu.VMEM((heads, 2, T, HD), BF16),
            pltpu.VMEM((HD, QB), F32),
            pltpu.VMEM((8, HD), F32),
            pltpu.VMEM((dp_size, 8, HD), F32),
            pltpu.VMEM((inner, 8, HD), F32),
            pltpu.VMEM((outer, 8, HD), F32),
            dma((heads, 4)),
            dma((heads, 4)),
            dma((heads, 2)),
            dma((heads, 2)),
            dma((heads,)),
            dma((heads,)),
            dma((heads,)),
            dma((heads,)),
            dma((heads,)),
            dma((heads,)),
            dma((exchanges,)),
            dma((exchanges,)),
        ],
        compiler_params=pltpu.CompilerParams(
            collective_id=0, has_side_effects=True, vmem_limit_bytes=VMEM_LIMIT
        ),
    )(
        query_raw[0],
        key_raw[0],
        values[0],
        out_grad[0],
        query_scale.reshape(1, HD),
        key_scale.reshape(1, HD),
        block_doc,
        doc_end,
    )
    return (
        attended[None],
        query_grad[None],
        key_grad[None],
        value_grad[None],
        query_gain.reshape(HD),
        key_gain.reshape(HD),
    )


def solution(mesh):
    ctx_size = mesh.shape["ctx"]
    dp_size = mesh.shape["dp"]
    inner = 4 if ctx_size % 4 == 0 else 1
    row = P("dp", "ctx", None)
    return jax.shard_map(
        functools.partial(body, (ctx_size, dp_size, inner)),
        mesh=mesh,
        in_specs=(row, row, row, row, P(), P(), P("dp", None), P("dp", None)),
        out_specs=(row, row, row, row, P(), P()),
        check_vma=False,
    )
```

time: 632 us -> 156 us (0.25); the launches traced: 621 us -> 156 us
  matrix products: 166 us -> 0 us
  local copies, waits for them, and re-layouts: 167 us -> 12.7 us
  Pallas kernels: 0 us -> 142 us
  blocking collectives: 112 us -> 0 us
  other arithmetic: 88.2 us -> 0 us
  waiting for transfers between devices: 58.3 us -> 0 us
  starting transfers between devices: 24 us -> 0 us
    dot_general x48 -> x0, matrix products: 166 us -> none  [the longest x16 56.9 us: dot_cols(): lax.dot_general(former, latter, (((0,), (0,)), ((), ())), preferred_eleme...]
    pallas_call x0 -> x1, Pallas kernels: none -> 142 us  [body(): pl.pallas_call(functools.partial(kernel, heads, ctx_size, dp_size, inner)...]
    psum x1 -> x0, blocking collectives: 112 us -> none  [body(): lax.psum((jnp.sum(query_scale_part.reshape(1, head_dim), axis=0), jnp.sum...]
    ppermute x8 -> x0, waiting for transfers between devices: 58.3 us -> none  [shifted(): return lax.ppermute(block, axis, route)]
    dot_general x16 -> x0, local copies, waits for them, and re-layouts: 48.4 us -> none  [dot_cols(): lax.dot_general(former, latter, (((0,), (0,)), ((), ())), preferred_eleme...]
    reduce_sum x23 -> x0, other arithmetic: 37.6 us -> none  [the longest x3 15.2 us: head_norm(): return inputs * lax.rsqrt(mean_square + norm_eps) * scales]
    reshape x6 -> x0, local copies, waits for them, and re-layouts: 26.8 us -> none  [the longest x2 9.74 us: body(): attended_heads.reshape(key_heads, group_size, tile_rows, head_dim)]
    ppermute x8 -> x0, starting transfers between devices: 24 us -> none  [shifted(): return lax.ppermute(block, axis, route)]
  transfers between devices with their start and end apart: 8 -> 0, of which waited for: 2 -> 0; matrix products, arithmetic and copies ran while one was open for 17% -> 0% of each run, Pallas kernels for 0% -> 0%
where the time goes in v1:
time: 156 us
  Pallas kernels  142 us (91%)
  local copies, waits for them, and re-layouts  12.7 us (8%)
    pallas_call x1, Pallas kernels, body(): pl.pallas_call(functools.partial(kernel, heads, ctx_size, dp_size, inner)...  142 us
    unnamed x20, local copies, waits for them, and re-layouts  12.7 us

profile of v1, /device:TPU:0, one launch (start us, length us, event | category | flops | bytes accessed | tf_op | source)
XLA Modules:
  0.0 155.8 jit_solution(17238846008584155952)
XLA Ops:
  0.6 0.0 copy-start
  0.6 1.2 copy-done
  1.9 0.0 copy-start.1
  1.9 1.2 copy-done.1
  3.1 0.0 copy-start.2
  3.1 0.7 copy-done.2
  3.7 0.0 copy-start.3
  3.7 0.7 copy-done.3
  4.4 0.0 copy-start.4
  4.4 0.7 copy-done.4
  5.1 0.0 copy-start.5
  5.1 0.7 copy-done.5
  5.7 142.5 %shard_map.127 = (bf16[512,2048]{1,0:T(8,128)(2,1)}, bf16[512,2048]{1,0:T(8,128)(2,1)}, bf16[512,1024]{1,0:T(8,128)(2,1)S(1)}, bf16[512,1024]{1,0:T(8,128)(2,1)S...) custom-call(bf16[512,2048]{1,0:T(8,128)(2,1)} %bitcast.20, bf16[512,1024]{1,0:T(8,128)(2,1)S(1)} %bitcast.14, ...), custom_call_target="tpu_custom_call" | custom-call | tf_op jit(solution)/shard_map/pallas_call | solution.py:407
  148.2 0.0 copy-start.6
  148.2 3.3 %copy.20 = bf16[1,512,2048]{2,1,0:T(8,128)(2,1)} copy(bf16[1,512,2048]{2,1,0:T(8,128)(2,1)} %bitcast.23) | data formatting | bytes 4194304
  151.5 0.0 copy-done.6
  151.5 1.3 copy.21
  152.9 1.0 copy.22
  153.8 1.0 copy.23
  154.8 0.5 copy.24
  155.3 0.5 copy.25
Async XLA Ops:
  0.6 1.2 copy-start
  1.9 1.2 copy-start.1
  3.1 0.7 copy-start.2
  3.7 0.7 copy-start.3
  4.4 0.7 copy-start.4
  5.1 0.7 copy-start.5
  148.2 3.3 %copy-start.6 = (bf16[512,2048]{1,0:T(8,128)(2,1)S(1)}, bf16[512,2048]{1,0:T(8,128)(2,1)}, u32[]{:S(2)}) copy-start(bf16[512,2048]{1,0:T(8,128)(2,1)} %get-tuple-element.13) | copy-start | bytes 6291460

commit v2 on v1

--- a/solution.py
+++ b/solution.py
@@ -23,7 +23,9 @@
 QB = 256
 KB = 256
 SPAN = WINDOW + QB
-VMEM_LIMIT = 48 * 1024 * 1024
+VMEM_LIMIT = 44 * 1024 * 1024
+NEAR_AHEAD = 3
+FINISH_LAG = 3
 
 
 def dot(a, b):
@@ -43,16 +45,15 @@
     k_hbm,
     v_hbm,
     do_hbm,
-    qs_ref,
-    ks_ref,
-    doc_ref,
-    end_ref,
+    qs_hbm,
+    ks_hbm,
+    doc_hbm,
+    end_hbm,
     att_hbm,
     dq_hbm,
     dk_hbm,
     dv_hbm,
-    qsg_ref,
-    ksg_ref,
+    gains_hbm,
     qbuf,
     dobuf,
     kvbuf,
@@ -78,7 +79,10 @@
     ksacc,
     ar1,
     ar2,
-    ar3,
+    gains,
+    scales,
+    docs,
+    small_sem,
     load_sem,
     store_sem,
     a_send,
@@ -96,6 +100,7 @@
     dp = lax.axis_index("dp")
     nxt = lax.rem(me + 1, ctx_size)
     prv = lax.rem(me + ctx_size - 1, ctx_size)
+    last = heads - 1
     outer = ctx_size // inner
     me_in = lax.rem(me, inner)
     me_out = me // inner
@@ -129,35 +134,49 @@
             src_ref=src, dst_ref=dst, send_sem=send, recv_sem=recv, device_id=device, device_id_type=MESH
         )
 
-    def halo_near(h):
+    def halo_near(h, half):
         narrow = pl.ds(pl.multiple_of(h * HD, HD), HD)
-        near = pl.ds(T, T)
-        return (
-            remote(k_hbm.at[:, narrow], kvbuf.at[h, 0, near], a_send.at[h, 0], a_recv.at[h, 0], {"ctx": nxt}),
-            remote(v_hbm.at[:, narrow], kvbuf.at[h, 1, near], a_send.at[h, 1], a_recv.at[h, 1], {"ctx": nxt}),
-        )
-
-    def halo_far(h):
+        source = pl.ds(half * QB, QB)
+        place = pl.ds(T + half * QB, QB)
+        return [
+            remote(
+                hbm.at[source, narrow],
+                kvbuf.at[h, kv, place],
+                a_send.at[h, half, kv],
+                a_recv.at[h, half, kv],
+                {"ctx": nxt},
+            )
+            for kv, hbm in enumerate((k_hbm, v_hbm))
+        ]
+
+    def halo_far(h, half):
         return remote(
-            kvbuf.at[h, :, pl.ds(T, T)], kvbuf.at[h, :, pl.ds(0, T)], r_send.at[h], r_recv.at[h], {"ctx": nxt}
-        )
-
-    def grad_far(h):
-        return remote(g2send.at[h], g2recv.at[h], g2_send.at[h], g2_recv.at[h], {"ctx": prv})
-
-    def grad_near(h):
-        return remote(g1buf.at[h], g1recv.at[h], g1_send.at[h], g1_recv.at[h], {"ctx": prv})
+            kvbuf.at[h, :, pl.ds(T + half * QB, QB)],
+            kvbuf.at[h, :, pl.ds(half * QB, QB)],
+            r_send.at[h, half],
+            r_recv.at[h, half],
+            {"ctx": nxt},
+        )
+
+    def grad_far(h, kv):
+        return remote(g2send.at[h, kv], g2recv.at[h, kv], g2_send.at[h, kv], g2_recv.at[h, kv], {"ctx": prv})
+
+    def grad_near(h, kv):
+        return remote(g1buf.at[h, kv], g1recv.at[h, kv], g1_send.at[h, kv], g1_recv.at[h, kv], {"ctx": prv})
 
     def partners(stage):
         if stage == 0:
-            return [{"dp": lax.rem(dp + d, dp_size)} for d in range(1, dp_size)]
-        if stage == 1:
-            return [{"ctx": me_out * inner + lax.rem(me_in + d, inner)} for d in range(1, inner)]
+            return [
+                {"dp": lax.rem(dp + d, dp_size), "ctx": me_out * inner + lax.rem(me_in + c, inner)}
+                for d in range(dp_size)
+                for c in range(inner)
+                if d or c
+            ]
         return [{"ctx": lax.rem(me_out + d, outer) * inner + me_in} for d in range(1, outer)]
 
-    stage_slot = (dp, me_in, me_out)
-    stage_buf = (ar1, ar2, ar3)
-    stage_base = (0, dp_size - 1, dp_size + inner - 2)
+    stage_slot = (dp * inner + me_in, me_out)
+    stage_buf = (ar1, ar2)
+    stage_base = (0, dp_size * inner - 1)
 
     def stage_copies(stage):
         slot = stage_buf[stage].at[stage_slot[stage]]
@@ -180,6 +199,15 @@
             total = total + stage_buf[stage][slot]
         return total
 
+    small_copies = (
+        pltpu.make_async_copy(qs_hbm, scales.at[pl.ds(0, 1)], small_sem.at[0]),
+        pltpu.make_async_copy(ks_hbm, scales.at[pl.ds(1, 1)], small_sem.at[1]),
+        pltpu.make_async_copy(doc_hbm, docs.at[pl.ds(0, 1)], small_sem.at[2]),
+        pltpu.make_async_copy(end_hbm, docs.at[pl.ds(1, 1)], small_sem.at[3]),
+    )
+    for copy in small_copies:
+        copy.start()
+
     def start_loads(h, carry):
         for copy in load_copies(h):
             copy.start()
@@ -188,54 +216,54 @@
     lax.fori_loop(0, heads, start_loads, 0)
 
     barrier = pltpu.get_barrier_semaphore()
-    greeted = [{"ctx": nxt}, {"ctx": prv}] + partners(0) + partners(1) + partners(2)
+    greeted = [{"ctx": nxt}, {"ctx": prv}] + partners(0) + partners(1)
     for device in greeted:
         pl.semaphore_signal(barrier, inc=1, device_id=device, device_id_type=MESH)
     pl.semaphore_wait(barrier, len(greeted))
 
     def start_halo(h):
-        for copy in halo_near(h):
-            copy.start()
-
-    for h in range(min(3, heads)):
+        for half in (1, 0):
+            for copy in halo_near(h, half):
+                copy.start()
+
+    def relay(h):
+        for half in (1, 0):
+            for copy in halo_near(h, half):
+                copy.wait_recv()
+            halo_far(h, half).start()
+
+    start_halo(0)
+    relay(0)
+    for h in range(1, min(NEAR_AHEAD, heads)):
         start_halo(h)
 
-    qrow = qs_ref[...]
-    krow = ks_ref[...]
+    for copy in small_copies:
+        copy.wait()
+    qrow = scales[0:1, :]
+    krow = scales[1:2, :]
     half = jnp.transpose(jnp.broadcast_to(qrow, (HD, HD)))
     qst[...] = jnp.concatenate([half, half], axis=1)
     qsacc[...] = jnp.zeros_like(qsacc)
     ksacc[...] = jnp.zeros_like(ksacc)
 
     block = me * T // BLOCK
-    doc = doc_ref[0, block]
-    before = doc_ref[0, jnp.maximum(block - 1, 0)]
+    doc = docs[0, block]
+    before = docs[0, jnp.maximum(block - 1, 0)]
     same = (block > 0) & (doc == before)
     into = me * T - block * BLOCK
     first = jnp.where(same, 0, 2 * T - into)
-    limit = end_ref[0, doc] - (me - 2) * T
-
-    def relay(h):
-        for copy in halo_near(h):
-            copy.wait_recv()
-        halo_far(h).start()
-
-    relay(0)
-
-    def prepare(h):
-        def prep_block(b, carry):
-            rows = pl.ds(pl.multiple_of(b * KB, KB), KB)
-            x = kvbuf[h, 0, rows, :].astype(F32)
-            mean_square = jnp.mean(x * x, axis=1, keepdims=True)
-            hat = x * lax.rsqrt(mean_square + norm_eps)
-            khat[rows, :] = hat
-            normed = (hat * krow).astype(BF16)
-            kn[rows, :] = normed
-            knt[:, rows] = jnp.transpose(normed)
-            vt[:, rows] = jnp.transpose(kvbuf[h, 1, rows, :])
-            return carry
-
-        lax.fori_loop(0, 3 * T // KB, prep_block, 0)
+    limit = docs[1, doc] - (me - 2) * T
+
+    def prepare(h, b):
+        rows = slice(b * KB, (b + 1) * KB)
+        x = kvbuf[h, 0, rows, :].astype(F32)
+        mean_square = jnp.mean(x * x, axis=1, keepdims=True)
+        hat = x * lax.rsqrt(mean_square + norm_eps)
+        khat[rows, :] = hat
+        normed = (hat * krow).astype(BF16)
+        kn[rows, :] = normed
+        knt[:, rows] = jnp.transpose(normed)
+        vt[:, rows] = jnp.transpose(kvbuf[h, 1, rows, :])
 
     def unit(h, g, j):
         rows = pl.ds(j * QB, QB)
@@ -281,15 +309,14 @@
         dqt = dot(knt[:, k0 : k0 + SPAN], ds_buf[...])
         dk = dot(ds_buf[...], jnp.transpose(qt))
         dv = dot(p_buf[...], do)
-        if g == 0 and j == 0:
-            dkacc[0:SPAN, :] = dk
-            dvacc[0:SPAN, :] = dv
+        if g == 0 and j == 1:
+            dkacc[k0 : k0 + SPAN, :] = dk
+            dvacc[k0 : k0 + SPAN, :] = dv
         elif g == 0:
-            old = SPAN - QB
-            dkacc[k0 : k0 + old, :] += dk[:old]
-            dvacc[k0 : k0 + old, :] += dv[:old]
-            dkacc[k0 + old : k0 + SPAN, :] = dk[old:]
-            dvacc[k0 + old : k0 + SPAN, :] = dv[old:]
+            dkacc[0:QB, :] = dk[:QB]
+            dvacc[0:QB, :] = dv[:QB]
+            dkacc[QB:SPAN, :] += dk[QB:]
+            dvacc[QB:SPAN, :] += dv[QB:]
         else:
             dkacc[k0 : k0 + SPAN, :] += dk
             dvacc[k0 : k0 + SPAN, :] += dv
@@ -300,10 +327,11 @@
         qsacc[...] += dqt * xr
 
     def send_parts(h):
+        g2send[h, 1] = dvacc[0:T, :].astype(BF16)
+        grad_far(h, 1).start()
         far_k = dkacc[0:T, :].astype(BF16)
         g2send[h, 0] = far_k
-        g2send[h, 1] = dvacc[0:T, :].astype(BF16)
-        grad_far(h).start()
+        grad_far(h, 0).start()
         near_k = dkacc[T : 2 * T, :].astype(BF16)
         g1buf[h, 0] = near_k
         g1buf[h, 1] = dvacc[T : 2 * T, :].astype(BF16)
@@ -317,49 +345,70 @@
         )
 
     def merge(h):
-        grad_far(h).wait_recv()
-        g1buf[h] = (g1buf[h].astype(F32) + g2recv[h].astype(F32)).astype(BF16)
-        grad_near(h).start()
+        for kv in (1, 0):
+            grad_far(h, kv).wait_recv()
+            g1buf[h, kv] = (g1buf[h, kv].astype(F32) + g2recv[h, kv].astype(F32)).astype(BF16)
+            grad_near(h, kv).start()
 
     def finish(h):
-        grad_near(h).wait_recv()
+        grad_near(h, 1).wait_recv()
         dkvout[h, 1] = (own[h, 1] + g1recv[h, 1].astype(F32)).astype(BF16)
-        grad = own[h, 0] + g1recv[h, 0].astype(F32)
+        grad_near(h, 0).wait_recv()
+        total_k = own[h, 0] + g1recv[h, 0].astype(F32)
         x = kvbuf[h, 0, pl.ds(2 * T, T), :].astype(F32)
         r = lax.rsqrt(jnp.mean(x * x, axis=1, keepdims=True) + norm_eps)
-        gs = grad * krow
+        gs = total_k * krow
         lean = jnp.mean(gs * x, axis=1, keepdims=True)
         dkvout[h, 0] = (gs * r - x * (r * r * r * lean)).astype(BF16)
         for copy in key_stores(h):
             copy.start()
 
+    def hand_on(h):
+        @pl.when(h + 1 < heads)
+        def _():
+            relay(h + 1)
+
+        @pl.when(h + NEAR_AHEAD < heads)
+        def _():
+            start_halo(h + NEAR_AHEAD)
+
     def step(h, carry):
-        @pl.when(h + 1 < heads)
-        def _():
-            relay(h + 1)
-
-        @pl.when(h + 3 < heads)
-        def _():
-            start_halo(h + 3)
-
         for copy in load_copies(h):
             copy.wait()
-        halo_far(h).wait_recv()
-        prepare(h)
-        for g in range(2):
-            for j in range(T // QB):
-                unit(h, g, j)
+        halo_far(h, 1).wait_recv()
+
+        @pl.when(h > 0)
+        def _():
+            hand_on(h)
+
+        for b in range(1, 3 * T // KB):
+            prepare(h, b)
+        unit(h, 0, 1)
+        unit(h, 1, 1)
+
+        @pl.when(h == last)
+        def _():
+            merge(h - 1)
+
+        halo_far(h, 0).wait_recv()
+        prepare(h, 0)
+        unit(h, 0, 0)
+        unit(h, 1, 0)
         send_parts(h)
         for copy in query_stores(h):
             copy.start()
 
-        @pl.when(h >= 1)
+        @pl.when(h == 0)
+        def _():
+            hand_on(h)
+
+        @pl.when((h >= 1) & (h < last))
         def _():
             merge(h - 1)
 
-        @pl.when(h >= 2)
-        def _():
-            finish(h - 2)
+        @pl.when(h >= FINISH_LAG)
+        def _():
+            finish(h - FINISH_LAG)
 
         return carry
 
@@ -369,46 +418,76 @@
     key_part = jnp.sum(ksacc[...], axis=0, keepdims=True)
     row = lax.broadcasted_iota(jnp.int32, (8, HD), 0)
     stage_start(0, jnp.where(row == 0, query_part, jnp.where(row == 1, key_part, 0.0)))
-    merge(heads - 1)
-    finish(heads - 2)
+    for h in range(heads - FINISH_LAG, heads - 2):
+        finish(h)
+    merge(last)
+    finish(last - 1)
     stage_start(1, stage_sum(0))
-    stage_start(2, stage_sum(1))
-    finish(heads - 1)
-    totals = stage_sum(2)
-    qsg_ref[...] = totals[0:1]
-    ksg_ref[...] = totals[1:2]
+    gains[...] = stage_sum(1)
+    gains_copy = pltpu.make_async_copy(gains, gains_hbm, small_sem.at[0])
+    gains_copy.start()
+    finish(last)
 
     def drain(h, carry):
-        for copy in halo_near(h):
-            copy.wait_send()
-        halo_far(h).wait_send()
-        grad_far(h).wait_send()
-        grad_near(h).wait_send()
+        for half in range(2):
+            for copy in halo_near(h, half):
+                copy.wait_send()
+            halo_far(h, half).wait_send()
+            grad_far(h, half).wait_send()
+            grad_near(h, half).wait_send()
         for copy in query_stores(h) + key_stores(h):
             copy.wait()
         return carry
 
     lax.fori_loop(0, heads, drain, 0)
+    gains_copy.wait()
+
+
+def flush(*refs):
+    sources, targets, sem = refs[:5], refs[5:11], refs[11]
+    copies = [
+        pltpu.make_async_copy(source, target, sem.at[i])
+        for i, (source, target) in enumerate(zip(sources[:4], targets[:4]))
+    ]
+    copies.append(pltpu.make_async_copy(sources[4].at[pl.ds(0, 1)], targets[4], sem.at[4]))
+    copies.append(pltpu.make_async_copy(sources[4].at[pl.ds(1, 1)], targets[5], sem.at[5]))
+    for copy in copies:
+        copy.start()
+    for copy in copies:
+        copy.wait()
 
 
 def body(mesh_shape, query_raw, key_raw, values, out_grad, query_scale, key_scale, block_doc, doc_end):
     ctx_size, dp_size, inner = mesh_shape
     tokens = query_raw.shape[1]
+    blocks = block_doc.shape[1]
     heads = key_raw.shape[2] // HD
     outer = ctx_size // inner
-    exchanges = dp_size + inner + outer - 3
+    exchanges = dp_size * inner + outer - 2
     any_spec = pl.BlockSpec(memory_space=pl.ANY)
-    vmem_spec = pl.BlockSpec(memory_space=pltpu.VMEM)
-    smem_spec = pl.BlockSpec(memory_space=pltpu.SMEM)
+    hbm_spec = pl.BlockSpec(memory_space=pltpu.HBM)
     dma = pltpu.SemaphoreType.DMA
     wide = jax.ShapeDtypeStruct((tokens, 2 * heads * HD), BF16)
     narrow = jax.ShapeDtypeStruct((tokens, heads * HD), BF16)
     gain = jax.ShapeDtypeStruct((1, HD), F32)
-    attended, query_grad, key_grad, value_grad, query_gain, key_gain = pl.pallas_call(
+    inputs = [
+        pltpu.with_memory_space_constraint(x, pltpu.HBM)
+        for x in (
+            query_raw[0],
+            key_raw[0],
+            values[0],
+            out_grad[0],
+            query_scale.reshape(1, HD),
+            key_scale.reshape(1, HD),
+            block_doc,
+            doc_end,
+        )
+    ]
+    results = pl.pallas_call(
         functools.partial(kernel, heads, ctx_size, dp_size, inner),
-        out_shape=(wide, wide, narrow, narrow, gain, gain),
-        in_specs=[any_spec] * 4 + [vmem_spec] * 2 + [smem_spec] * 2,
-        out_specs=[any_spec] * 4 + [vmem_spec] * 2,
+        out_shape=(wide, wide, narrow, narrow, jax.ShapeDtypeStruct((8, HD), F32)),
+        in_specs=[hbm_spec] * 8,
+        out_specs=[any_spec] * 5,
         scratch_shapes=[
             pltpu.VMEM((heads, T, 2 * HD), BF16),
             pltpu.VMEM((heads, T, 2 * HD), BF16),
@@ -433,35 +512,37 @@
             pltpu.VMEM((heads, 2, T, HD), BF16),
             pltpu.VMEM((HD, QB), F32),
             pltpu.VMEM((8, HD), F32),
-            pltpu.VMEM((dp_size, 8, HD), F32),
-            pltpu.VMEM((inner, 8, HD), F32),
+            pltpu.VMEM((dp_size * inner, 8, HD), F32),
             pltpu.VMEM((outer, 8, HD), F32),
+            pltpu.VMEM((8, HD), F32),
+            pltpu.VMEM((2, HD), F32),
+            pltpu.SMEM((2, blocks), jnp.int32),
+            dma((4,)),
             dma((heads, 4)),
             dma((heads, 4)),
+            dma((heads, 2, 2)),
+            dma((heads, 2, 2)),
             dma((heads, 2)),
             dma((heads, 2)),
-            dma((heads,)),
-            dma((heads,)),
-            dma((heads,)),
-            dma((heads,)),
-            dma((heads,)),
-            dma((heads,)),
+            dma((heads, 2)),
+            dma((heads, 2)),
+            dma((heads, 2)),
+            dma((heads, 2)),
             dma((exchanges,)),
             dma((exchanges,)),
         ],
         compiler_params=pltpu.CompilerParams(
             collective_id=0, has_side_effects=True, vmem_limit_bytes=VMEM_LIMIT
         ),
-    )(
-        query_raw[0],
-        key_raw[0],
-        values[0],
-        out_grad[0],
-        query_scale.reshape(1, HD),
-        key_scale.reshape(1, HD),
-        block_doc,
-        doc_end,
-    )
+    )(*inputs)
+    attended, query_grad, key_grad, value_grad, query_gain, key_gain = pl.pallas_call(
+        flush,
+        out_shape=(wide, wide, narrow, narrow, gain, gain),
+        in_specs=[any_spec] * 5,
+        out_specs=[any_spec] * 6,
+        scratch_shapes=[dma((6,))],
+        compiler_params=pltpu.CompilerParams(vmem_limit_bytes=1024 * 1024),
+    )(*results)
     return (
         attended[None],
         query_grad[None],

time: 156 us -> 138 us (0.88)
  local copies, waits for them, and re-layouts: 12.7 us -> 0 us
  Pallas kernels: 142 us -> 137 us
    unnamed x20 -> x0, local copies, waits for them, and re-layouts: 12.7 us -> none
    pallas_call x1, Pallas kernels: 142 us -> 134 us  [body(): pl.pallas_call(functools.partial(kernel, heads, ctx_size, dp_size, inner)...]
    pallas_call x0 -> x1, Pallas kernels: none -> 2.73 us  [body(): pl.pallas_call(flush, out_shape=(wide, wide, narrow, narrow, gain, gain),...]
where the time goes in v2:
time: 138 us
  Pallas kernels  137 us (99%)
    pallas_call x1, Pallas kernels, body(): pl.pallas_call(functools.partial(kernel, heads, ctx_size, dp_size, inner)...  134 us

profile of v2, /device:TPU:0, one launch (start us, length us, event | category | flops | bytes accessed | tf_op | source)
XLA Modules:
  0.0 137.7 jit_solution(4543499896216736251)
XLA Ops:
  0.6 134.3 %shard_map.127 = (bf16[512,2048]{1,0:T(8,128)(2,1)S(1)}, bf16[512,2048]{1,0:T(8,128)(2,1)S(1)}, bf16[512,1024]{1,0:T(8,128)(2,1)S(1)}, bf16[512,1024]{1,0:T(8,128)(2,1)S(1)}, f32[8,128]{1,0:T(8,128)S(1)}) custom-call(bf16[512,2048]{1,0:T(8,128)(2,1)} %bitcast.12, bf16[512,1024]{1,0:T(8,128)(2,1)} %bitcast.14, bf16[512,1024]{1,0:T(8,128)(2,1)} %bitcast.15, ...), custom_call_target="tpu_custom_call" | custom-call | tf_op jit(solution)/shard_map/pallas_call | solution.py:486
  135.0 2.7 %shard_map.128 = (bf16[512,2048]{1,0:T(8,128)(2,1)}, bf16[512,2048]{1,0:T(8,128)(2,1)}, bf16[512,1024]{1,0:T(8,128)(2,1)}, bf16[512,1024]{1,0:T(8,128)(2,1)}, f32[1,128]{1,0:T(1,128)}, /*index=5*/f32[1,128]{1,0:T(1,128)}) custom-call(bf16[512,2048]{1,0:T(8,128)(2,1)S(1)} %get-tuple-element.17.refs_0_, bf16[512,2048]{1,0:T(8,128)(2,1)S(1)} %get-tuple-element.18.refs_1_, ...), custom_call_target="tpu_custom_call" | custom-call | tf_op jit(solution)/shard_map/pallas_call | solution.py:538

commit v3 on v2

--- a/solution.py
+++ b/solution.py
@@ -23,7 +23,7 @@
 QB = 256
 KB = 256
 SPAN = WINDOW + QB
-VMEM_LIMIT = 44 * 1024 * 1024
+VMEM_LIMIT = 46 * 1024 * 1024
 NEAR_AHEAD = 3
 FINISH_LAG = 3
 
@@ -265,84 +265,103 @@
         knt[:, rows] = jnp.transpose(normed)
         vt[:, rows] = jnp.transpose(kvbuf[h, 1, rows, :])
 
-    def unit(h, g, j):
+    def unit(h, g, j, kept):
         rows = pl.ds(j * QB, QB)
         cols = pl.ds(g * HD, HD)
+        lanes = slice(g * QB, (g + 1) * QB)
         k0 = j * QB
         nb = SPAN // KB
+        blocks = [slice(b * KB, (b + 1) * KB) for b in range(nb)]
         gain = qst[...]
         xt = jnp.transpose(qbuf[h, rows, cols].astype(F32))
         mean_square = jnp.mean(xt * xt, axis=0, keepdims=True)
         r = lax.rsqrt(mean_square + norm_eps)
-        xr = xt * r
-        qt = (xr * gain).astype(BF16)
-        do = dobuf[h, rows, cols]
-        dot_t = jnp.transpose(do)
+        qt = (xt * r * gain).astype(BF16)
+        dot_t = jnp.transpose(dobuf[h, rows, cols])
+        kept.append(jnp.transpose(qt))
         lane = lax.broadcasted_iota(jnp.int32, (1, QB), 1)
         low = jnp.maximum(first, k0 + 1 + lane)
         high = jnp.minimum(limit, k0 + 1 + WINDOW + lane)
         place = lax.broadcasted_iota(jnp.int32, (KB, QB), 0)
         peak = jnp.full((8, QB), MASKED, F32)
         for b in range(nb):
-            keys = kn[k0 + b * KB : k0 + (b + 1) * KB, :]
-            s = dot(keys, qt)
+            s = dot(kn[k0 + b * KB : k0 + (b + 1) * KB, :], qt)
             spot = place + (k0 + b * KB)
             s = jnp.where((spot >= low) & (spot < high), s, MASKED)
-            s_buf[b * KB : (b + 1) * KB, :] = s
+            s_buf[blocks[b], lanes] = s
             peak = jnp.maximum(peak, fold_rows(s, jnp.max))
         peak = jnp.max(peak, axis=0, keepdims=True)
+        yield
         total = jnp.zeros((8, QB), F32)
         for b in range(nb):
-            e = jnp.exp2((s_buf[b * KB : (b + 1) * KB, :] - peak) * (score_scale * LOG2E))
-            s_buf[b * KB : (b + 1) * KB, :] = e
+            e = jnp.exp2((s_buf[blocks[b], lanes] - peak) * (score_scale * LOG2E))
+            s_buf[blocks[b], lanes] = e
             total = total + fold_rows(e, jnp.sum)
         inverse = 1.0 / jnp.sum(total, axis=0, keepdims=True)
         for b in range(nb):
-            p_buf[b * KB : (b + 1) * KB, :] = (s_buf[b * KB : (b + 1) * KB, :] * inverse).astype(BF16)
-        o = dot(vt[:, k0 : k0 + SPAN], p_buf[...]).astype(BF16)
+            p_buf[blocks[b], lanes] = (s_buf[blocks[b], lanes] * inverse).astype(BF16)
+        yield
+        o = dot(vt[:, k0 : k0 + SPAN], p_buf[:, lanes]).astype(BF16)
         attbuf[h, rows, cols] = jnp.transpose(o)
         delta = jnp.sum(dot_t.astype(F32) * o.astype(F32), axis=0, keepdims=True)
         for b in range(nb):
             part = dot(kvbuf[h, 1, k0 + b * KB : k0 + (b + 1) * KB, :], dot_t)
-            shares = s_buf[b * KB : (b + 1) * KB, :] * inverse
-            ds_buf[b * KB : (b + 1) * KB, :] = (shares * (part - delta) * score_scale).astype(BF16)
-        dqt = dot(knt[:, k0 : k0 + SPAN], ds_buf[...])
-        dk = dot(ds_buf[...], jnp.transpose(qt))
-        dv = dot(p_buf[...], do)
-        if g == 0 and j == 1:
+            shares = s_buf[blocks[b], lanes] * inverse
+            ds_buf[blocks[b], lanes] = (shares * (part - delta) * score_scale).astype(BF16)
+        yield
+        dqt = dot(knt[:, k0 : k0 + SPAN], ds_buf[:, lanes])
+        gs = dqt * gain
+        lean = jnp.mean(gs * xt, axis=0, keepdims=True)
+        dx = gs * r - xt * (r * r * r * lean)
+        dqbuf[h, rows, cols] = jnp.transpose(dx.astype(BF16))
+        qsacc[...] += dqt * (xt * r)
+        yield
+
+    def unit_pair(h, j):
+        rows = pl.ds(j * QB, QB)
+        k0 = j * QB
+        kept = []
+        one, two = unit(h, 0, j, kept), unit(h, 1, j, kept)
+        for stage in (one, two, one, one, two, two, one, two):
+            next(stage)
+        queries = jnp.concatenate(kept, axis=0)
+        grads = jnp.concatenate([dobuf[h, rows, 0:HD], dobuf[h, rows, HD : 2 * HD]], axis=0)
+        dv = dot(p_buf[...], grads)
+        dk = dot(ds_buf[...], queries)
+        if j == 1:
             dkacc[k0 : k0 + SPAN, :] = dk
             dvacc[k0 : k0 + SPAN, :] = dv
-        elif g == 0:
+        else:
             dkacc[0:QB, :] = dk[:QB]
             dvacc[0:QB, :] = dv[:QB]
             dkacc[QB:SPAN, :] += dk[QB:]
             dvacc[QB:SPAN, :] += dv[QB:]
-        else:
-            dkacc[k0 : k0 + SPAN, :] += dk
-            dvacc[k0 : k0 + SPAN, :] += dv
-        gs = dqt * gain
-        lean = jnp.mean(gs * xt, axis=0, keepdims=True)
-        dx = gs * r - xt * (r * r * r * lean)
-        dqbuf[h, rows, cols] = jnp.transpose(dx.astype(BF16))
-        qsacc[...] += dqt * xr
 
     def send_parts(h):
-        g2send[h, 1] = dvacc[0:T, :].astype(BF16)
-        grad_far(h, 1).start()
         far_k = dkacc[0:T, :].astype(BF16)
-        g2send[h, 0] = far_k
-        grad_far(h, 0).start()
         near_k = dkacc[T : 2 * T, :].astype(BF16)
-        g1buf[h, 0] = near_k
-        g1buf[h, 1] = dvacc[T : 2 * T, :].astype(BF16)
         own_k = dkacc[2 * T : 3 * T, :]
-        own[h, 0] = own_k
-        own[h, 1] = dvacc[2 * T : 3 * T, :]
         ksacc[...] += (
             fold_rows(far_k.astype(F32) * khat[0:T, :], jnp.sum)
             + fold_rows(near_k.astype(F32) * khat[T : 2 * T, :], jnp.sum)
             + fold_rows(own_k * khat[2 * T : 3 * T, :], jnp.sum)
         )
+        g2send[h, 1] = dvacc[0:T, :].astype(BF16)
+        g2send[h, 0] = far_k
+
+        @pl.when(h == last)
+        def _():
+            query_part = jnp.sum(jnp.transpose(qsacc[...]), axis=0, keepdims=True)
+            key_part = jnp.sum(ksacc[...], axis=0, keepdims=True)
+            row = lax.broadcasted_iota(jnp.int32, (8, HD), 0)
+            stage_start(0, jnp.where(row == 0, query_part, jnp.where(row == 1, key_part, 0.0)))
+
+        grad_far(h, 1).start()
+        grad_far(h, 0).start()
+        g1buf[h, 0] = near_k
+        g1buf[h, 1] = dvacc[T : 2 * T, :].astype(BF16)
+        own[h, 0] = own_k
+        own[h, 1] = dvacc[2 * T : 3 * T, :]
 
     def merge(h):
         for kv in (1, 0):
@@ -383,8 +402,7 @@
 
         for b in range(1, 3 * T // KB):
             prepare(h, b)
-        unit(h, 0, 1)
-        unit(h, 1, 1)
+        unit_pair(h, 1)
 
         @pl.when(h == last)
         def _():
@@ -392,8 +410,7 @@
 
         halo_far(h, 0).wait_recv()
         prepare(h, 0)
-        unit(h, 0, 0)
-        unit(h, 1, 0)
+        unit_pair(h, 0)
         send_parts(h)
         for copy in query_stores(h):
             copy.start()
@@ -414,15 +431,11 @@
 
     lax.fori_loop(0, heads, step, 0)
 
-    query_part = jnp.sum(jnp.transpose(qsacc[...]), axis=0, keepdims=True)
-    key_part = jnp.sum(ksacc[...], axis=0, keepdims=True)
-    row = lax.broadcasted_iota(jnp.int32, (8, HD), 0)
-    stage_start(0, jnp.where(row == 0, query_part, jnp.where(row == 1, key_part, 0.0)))
     for h in range(heads - FINISH_LAG, heads - 2):
         finish(h)
+    stage_start(1, stage_sum(0))
     merge(last)
     finish(last - 1)
-    stage_start(1, stage_sum(0))
     gains[...] = stage_sum(1)
     gains_copy = pltpu.make_async_copy(gains, gains_hbm, small_sem.at[0])
     gains_copy.start()
@@ -500,9 +513,9 @@
             pltpu.VMEM((HD, 3 * T), BF16),
             pltpu.VMEM((3 * T, HD), F32),
             pltpu.VMEM((HD, QB), F32),
-            pltpu.VMEM((SPAN, QB), F32),
-            pltpu.VMEM((SPAN, QB), BF16),
-            pltpu.VMEM((SPAN, QB), BF16),
+            pltpu.VMEM((SPAN, 2 * QB), F32),
+            pltpu.VMEM((SPAN, 2 * QB), BF16),
+            pltpu.VMEM((SPAN, 2 * QB), BF16),
             pltpu.VMEM((3 * T, HD), F32),
             pltpu.VMEM((3 * T, HD), F32),
             pltpu.VMEM((heads, 2, T, HD), F32),

time: 138 us -> 135 us (0.978)
  Pallas kernels: 137 us -> 134 us
    pallas_call x1, Pallas kernels: 134 us -> 131 us  [body(): pl.pallas_call(functools.partial(kernel, heads, ctx_size, dp_size, inner)...]
where the time goes in v3:
time: 135 us
  Pallas kernels  134 us (99%)
    pallas_call x1, Pallas kernels, body(): pl.pallas_call(functools.partial(kernel, heads, ctx_size, dp_size, inner)...  131 us
    pallas_call x1, Pallas kernels, body(): pl.pallas_call(flush, out_shape=(wide, wide, narrow, narrow, gain, gain),...  2.73 us

profile of v3, /device:TPU:0, one launch (start us, length us, event | category | flops | bytes accessed | tf_op | source)
XLA Modules:
  0.0 134.7 jit_solution(9904529484815732266)
XLA Ops:
  0.6 131.4 %shard_map.127 = (bf16[512,2048]{1,0:T(8,128)(2,1)S(1)}, bf16[512,2048]{1,0:T(8,128)(2,1)S(1)}, bf16[512,1024]{1,0:T(8,128)(2,1)S(1)}, bf16[512,1024]{1,0:T(8,128)(2,1)S(1)}, f32[8,128]{1,0:T(8,128)S(1)}) custom-call(bf16[512,2048]{1,0:T(8,128)(2,1)} %bitcast.12, bf16[512,1024]{1,0:T(8,128)(2,1)} %bitcast.14, bf16[512,1024]{1,0:T(8,128)(2,1)} %bitcast.15, ...), custom_call_target="tpu_custom_call" | custom-call | tf_op jit(solution)/shard_map/pallas_call | solution.py:499
  132.0 2.7 %shard_map.128 = (bf16[512,2048]{1,0:T(8,128)(2,1)}, bf16[512,2048]{1,0:T(8,128)(2,1)}, bf16[512,1024]{1,0:T(8,128)(2,1)}, bf16[512,1024]{1,0:T(8,128)(2,1)}, f32[1,128]{1,0:T(1,128)}, /*index=5*/f32[1,128]{1,0:T(1,128)}) custom-call(bf16[512,2048]{1,0:T(8,128)(2,1)S(1)} %get-tuple-element.17.refs_0_, bf16[512,2048]{1,0:T(8,128)(2,1)S(1)} %get-tuple-element.18.refs_1_, ...), custom_call_target="tpu_custom_call" | custom-call | tf_op jit(solution)/shard_map/pallas_call | solution.py:551

commit v4 on v3

--- a/solution.py
+++ b/solution.py
@@ -205,20 +205,18 @@
         pltpu.make_async_copy(doc_hbm, docs.at[pl.ds(0, 1)], small_sem.at[2]),
         pltpu.make_async_copy(end_hbm, docs.at[pl.ds(1, 1)], small_sem.at[3]),
     )
-    for copy in small_copies:
-        copy.start()
-
     def start_loads(h, carry):
         for copy in load_copies(h):
             copy.start()
         return carry
 
-    lax.fori_loop(0, heads, start_loads, 0)
-
     barrier = pltpu.get_barrier_semaphore()
     greeted = [{"ctx": nxt}, {"ctx": prv}] + partners(0) + partners(1)
     for device in greeted:
         pl.semaphore_signal(barrier, inc=1, device_id=device, device_id_type=MESH)
+    for copy in small_copies:
+        copy.start()
+    start_loads(0, 0)
     pl.semaphore_wait(barrier, len(greeted))
 
     def start_halo(h):
@@ -233,6 +231,7 @@
             halo_far(h, half).start()
 
     start_halo(0)
+    lax.fori_loop(1, heads, start_loads, 0)
     relay(0)
     for h in range(1, min(NEAR_AHEAD, heads)):
         start_halo(h)
@@ -404,7 +403,7 @@
             prepare(h, b)
         unit_pair(h, 1)
 
-        @pl.when(h == last)
+        @pl.when(h >= 1)
         def _():
             merge(h - 1)
 
@@ -419,10 +418,6 @@
         def _():
             hand_on(h)
 
-        @pl.when((h >= 1) & (h < last))
-        def _():
-            merge(h - 1)
-
         @pl.when(h >= FINISH_LAG)
         def _():
             finish(h - FINISH_LAG)
@@ -433,14 +428,6 @@
 
     for h in range(heads - FINISH_LAG, heads - 2):
         finish(h)
-    stage_start(1, stage_sum(0))
-    merge(last)
-    finish(last - 1)
-    gains[...] = stage_sum(1)
-    gains_copy = pltpu.make_async_copy(gains, gains_hbm, small_sem.at[0])
-    gains_copy.start()
-    finish(last)
-
     def drain(h, carry):
         for half in range(2):
             for copy in halo_near(h, half):
@@ -452,7 +439,16 @@
             copy.wait()
         return carry
 
-    lax.fori_loop(0, heads, drain, 0)
+    stage_start(1, stage_sum(0))
+    lax.fori_loop(0, heads - 2, drain, 0)
+    merge(last)
+    finish(last - 1)
+    gains[...] = stage_sum(1)
+    gains_copy = pltpu.make_async_copy(gains, gains_hbm, small_sem.at[0])
+    gains_copy.start()
+    finish(last)
+
+    lax.fori_loop(heads - 2, heads, drain, 0)
     gains_copy.wait()
 
 

time: 135 us -> 133 us (0.985)
  Pallas kernels: 134 us -> 132 us
    pallas_call x1, Pallas kernels: 131 us -> 129 us  [body(): pl.pallas_call(functools.partial(kernel, heads, ctx_size, dp_size, inner)...]
where the time goes in v4:
time: 133 us
  Pallas kernels  132 us (99%)
    pallas_call x1, Pallas kernels, body(): pl.pallas_call(functools.partial(kernel, heads, ctx_size, dp_size, inner)...  129 us
    pallas_call x1, Pallas kernels, body(): pl.pallas_call(flush, out_shape=(wide, wide, narrow, narrow, gain, gain),...  2.73 us

profile of v4, /device:TPU:0, one launch (start us, length us, event | category | flops | bytes accessed | tf_op | source)
XLA Modules:
  0.0 132.7 jit_solution(1005986153348146117)
XLA Ops:
  0.6 129.4 %shard_map.127 = (bf16[512,2048]{1,0:T(8,128)(2,1)S(1)}, bf16[512,2048]{1,0:T(8,128)(2,1)S(1)}, bf16[512,1024]{1,0:T(8,128)(2,1)S(1)}, bf16[512,1024]{1,0:T(8,128)(2,1)S(1)}, f32[8,128]{1,0:T(8,128)S(1)}) custom-call(bf16[512,2048]{1,0:T(8,128)(2,1)} %bitcast.12, bf16[512,1024]{1,0:T(8,128)(2,1)} %bitcast.14, bf16[512,1024]{1,0:T(8,128)(2,1)} %bitcast.15, ...), custom_call_target="tpu_custom_call" | custom-call | tf_op jit(solution)/shard_map/pallas_call | solution.py:495
  130.0 2.7 %shard_map.128 = (bf16[512,2048]{1,0:T(8,128)(2,1)}, bf16[512,2048]{1,0:T(8,128)(2,1)}, bf16[512,1024]{1,0:T(8,128)(2,1)}, bf16[512,1024]{1,0:T(8,128)(2,1)}, f32[1,128]{1,0:T(1,128)}, /*index=5*/f32[1,128]{1,0:T(1,128)}) custom-call(bf16[512,2048]{1,0:T(8,128)(2,1)S(1)} %get-tuple-element.17.refs_0_, bf16[512,2048]{1,0:T(8,128)(2,1)S(1)} %get-tuple-element.18.refs_1_, ...), custom_call_target="tpu_custom_call" | custom-call | tf_op jit(solution)/shard_map/pallas_call | solution.py:547

commit v5 on v4

--- a/solution.py
+++ b/solution.py
@@ -24,7 +24,7 @@
 KB = 256
 SPAN = WINDOW + QB
 VMEM_LIMIT = 46 * 1024 * 1024
-NEAR_AHEAD = 3
+NEAR_AHEAD = 4
 FINISH_LAG = 3
 
 

time: 133 us -> 139 us (1.045)
  Pallas kernels: 132 us -> 138 us
    pallas_call x1, Pallas kernels: 129 us -> 135 us  [body(): pl.pallas_call(functools.partial(kernel, heads, ctx_size, dp_size, inner)...]
where the time goes in v5:
time: 139 us; the launch traced here: 138 us
  Pallas kernels  138 us (99%)
    pallas_call x1, Pallas kernels, body(): pl.pallas_call(functools.partial(kernel, heads, ctx_size, dp_size, inner)...  135 us

profile of v5, /device:TPU:0, one launch (start us, length us, event | category | flops | bytes accessed | tf_op | source)
XLA Modules:
  0.0 138.3 jit_solution(17423900653369117748)
XLA Ops:
  0.6 134.9 %shard_map.127 = (bf16[512,2048]{1,0:T(8,128)(2,1)S(1)}, bf16[512,2048]{1,0:T(8,128)(2,1)S(1)}, bf16[512,1024]{1,0:T(8,128)(2,1)S(1)}, bf16[512,1024]{1,0:T(8,128)(2,1)S(1)}, f32[8,128]{1,0:T(8,128)S(1)}) custom-call(bf16[512,2048]{1,0:T(8,128)(2,1)} %bitcast.12, bf16[512,1024]{1,0:T(8,128)(2,1)} %bitcast.14, bf16[512,1024]{1,0:T(8,128)(2,1)} %bitcast.15, ...), custom_call_target="tpu_custom_call" | custom-call | tf_op jit(solution)/shard_map/pallas_call | solution.py:495
  135.6 2.7 %shard_map.128 = (bf16[512,2048]{1,0:T(8,128)(2,1)}, bf16[512,2048]{1,0:T(8,128)(2,1)}, bf16[512,1024]{1,0:T(8,128)(2,1)}, bf16[512,1024]{1,0:T(8,128)(2,1)}, f32[1,128]{1,0:T(1,128)}, /*index=5*/f32[1,128]{1,0:T(1,128)}) custom-call(bf16[512,2048]{1,0:T(8,128)(2,1)S(1)} %get-tuple-element.17.refs_0_, bf16[512,2048]{1,0:T(8,128)(2,1)S(1)} %get-tuple-element.18.refs_1_, ...), custom_call_target="tpu_custom_call" | custom-call | tf_op jit(solution)/shard_map/pallas_call | solution.py:547
